TPU v7x, 768 devices: a whole 4x8x12 slice. The times are simulated.
768 devices in a mesh: lon: 96 (over z, y_hi, x), colat: 8 (over y_lo, core).
Axes of the slice: x: 4, y: 8 (y_hi: 2, y_lo: 4; y = y_hi * 4 + y_lo), z: 12, core: 2. Of those that a mesh axis runs over, the one named last changes fastest.
Arguments:
- pattern: bfloat16 [192, 2, 128, 384], P('lon', None, 'colat'), may hold values from -6 to 6
- phi_filter: bfloat16 [384, 384], replicated, may hold values from -0.3125 to 0.3125
- trans_table: float32 [316, 2, 128, 384], P(None, None, None, 'lon'), may hold values from -0.66 to 0.66
- partners: int32 [192, 40], replicated, may hold values from 0 to 191
- op_index: int32 [192, 40], replicated, may hold values from 0 to 315
- anter_weight: float32 [17, 128], P(None, 'colat'), may hold values from -1.5 to 1.5
- return_boxes: int32 [96, 5], replicated, may hold values from 0 to 191, as said below
- return_count: int32 [96], P('lon'), may hold values from 1 to 5, as said below
- leaf_weight: bfloat16 [2, 128, 384, 256], P(None, 'colat'), may hold values from -0.01953125 to 0.01953125
Outputs:
- leaf_field: float32 [96, 5, 256], P('lon', None, 'colat')
Inputs may be any that keep to these rules, and one draw needn't show every extreme that they name: `return_boxes`: every box appears exactly once among the first return_count[j] entries of row j over all j; padded entries are 0. Some leaf owner receives exactly 5 boxes. `return_count`: the counts sum to 192.
All inputs are finite; a program needn't handle non-finite values.
Results may differ from a plain program's by a relative error of at most 0.0041.
Values may be sent and summed in bfloat16 or wider, within the bound.
A program may use at most 32 MiB of HBM per device.

v0:
```python
import functools

import jax
import jax.numpy as jnp
from jax import lax
from jax.experimental import pallas as pl
from jax.experimental.pallas import tpu as pltpu
from jax.sharding import PartitionSpec as P

F32, BF16, I32 = jnp.float32, jnp.bfloat16, jnp.int32
MESH = pl.DeviceIdType.MESH
EDGE = 8
X = 4
STEP = 40
UC = 32
RS_ROWS = 48


def dot(a, b):
    return jnp.dot(a, b, preferred_element_type=F32)


def dot_nt(a, b):
    return lax.dot_general(a, b, (((1,), (1,)), ((), ())), preferred_element_type=F32)


def split(x):
    hi = x.astype(BF16)
    return hi, (x - hi.astype(F32)).astype(BF16)


def iota(shape, axis):
    return lax.broadcasted_iota(I32, shape, axis)


def ones_where(mask):
    return jnp.where(mask, 1.0, 0.0).astype(F32)


def band(taps, first, offset, rows, phi_lane):
    along = jnp.concatenate([taps, jnp.zeros((112, 128), F32)], axis=0).T
    t_out = iota((128, 128), 0) & 15
    shift = t_out - (iota((128, 128), 1) + offset) + EDGE
    mixed = jnp.zeros((128, 128), F32)
    for s in range(2 * EDGE + 1):
        mixed = mixed + jnp.where(shift == s, along[s : s + 1, :], 0.0)
    wide = 32 * rows
    lane = iota((128, wide), 1)
    spread = ones_where(iota((128, wide), 0) == ((lane >> 4) & (rows - 1)) + first).astype(BF16)
    row = iota((128, wide), 0)
    same = (row >> 6) == (lane // (16 * rows))
    keep = ones_where(same & ((lane & 15) == phi_lane + ((row >> 4) & 3)))
    hi, lo = split(mixed)
    return (dot(hi, spread) * keep).astype(BF16), (dot(lo, spread) * keep).astype(BF16)


def kernel(
    lon,
    colat,
    pattern_hbm,
    phi_filter_hbm,
    partners_hbm,
    ops_hbm,
    taps_hbm,
    returns_hbm,
    count,
    table,
    weight,
    out,
    pattern,
    phi_filter,
    partners,
    ops,
    taps,
    returns,
    outbox,
    inbox,
    ybuf,
    tab,
    tcat_hi,
    tcat_lo,
    tab_t,
    src,
    place,
    fold,
    wide_ops,
    wide_partners,
    rcat,
    factors,
    picks,
    lw_own,
    lw_prev,
    lw_next,
    tapsbox,
    acc,
    rs_out,
    rs_in,
    gbd_hi,
    gbd_lo,
    ohret,
    outbox2,
    inbox2,
    load_sem,
    local_sem,
    halo_send,
    halo_recv,
    a_send,
    a_recv,
    rs_send,
    rs_recv,
    b_send,
    b_recv,
):
    i = lax.axis_index("lon")
    k = lax.axis_index("colat")
    prev_k = lax.rem(k + colat - 1, colat)
    next_k = lax.rem(k + 1, colat)
    nops8 = table.shape[0]
    theta = table.shape[1]
    npart = partners.shape[0]

    barrier = pltpu.get_barrier_semaphore()

    z_size = lon // (2 * X)
    here_z, here_y, here_x = lax.div(i, 2 * X), lax.rem(lax.div(i, X), 2), lax.rem(i, X)
    along_x = [lax.rem(here_x + offset, X) for offset in (2, 1, 3, 0)]

    def for_peers(act):
        for row, rings in (((1 - here_y) * X, z_size), (here_y * X, z_size - 1)):

            def ring(a, carry):
                step = ((a + 1) >> 1) * (1 - 2 * (a & 1))
                z = lax.rem(here_z + z_size // 2 + step, z_size)
                for x in along_x:
                    act(z * (2 * X) + row + x)
                return carry

            lax.fori_loop(0, rings, ring, 0)
        for x in along_x[:3]:
            act(here_z * (2 * X) + here_y * X + x)

    def greet(to):
        pl.semaphore_signal(barrier, inc=1, device_id={"lon": to}, device_id_type=MESH)

    def greet_colat(s, carry):
        pl.semaphore_signal(barrier, inc=1, device_id={"colat": lax.rem(k + s, colat)}, device_id_type=MESH)
        return carry

    for_peers(greet)
    lax.fori_loop(1, colat, greet_colat, 0)

    block = pl.multiple_of(lax.div(i, 4) * 16, 16)
    loads = [
        pltpu.make_async_copy(a, b, load_sem.at[n])
        for n, (a, b) in enumerate(
            (
                (phi_filter_hbm, phi_filter),
                (pattern_hbm, pattern),
                (taps_hbm, taps),
                (ops_hbm, ops),
                (partners_hbm, partners),
                (returns_hbm, returns),
            )
        )
    ]
    for load in loads:
        load.start()
    load_table = pltpu.make_async_copy(table, tab.at[pl.ds(0, nops8)], local_sem.at[0])
    load_table.start()
    load_lw = pltpu.make_async_copy(weight.at[:, :, pl.ds(block, 16), :], lw_own, local_sem.at[1])
    load_lw.start()

    for load in loads:
        load.wait()

    rows2 = jnp.concatenate([pattern[...], pattern[...]], axis=0)
    filtered = dot(rows2, phi_filter[...]).astype(BF16).astype(F32)
    ybuf[...] = filtered.T
    left = iota((lon, 128), 1) < 64
    for h in range(2):
        low = ybuf[pl.ds(2 * h, lon, stride=4), :]
        high = ybuf[pl.ds(2 * h + 1, lon, stride=4), :]
        outbox[:, h, :] = jnp.where(left, low, high)
    tapsbox[0, :, 0:17] = taps[...]

    pl.semaphore_wait(barrier, lon + colat - 2)

    def send_a(to):
        pltpu.make_async_remote_copy(
            src_ref=outbox.at[to],
            dst_ref=inbox.at[i],
            send_sem=a_send,
            recv_sem=a_recv,
            device_id={"lon": to},
            device_id_type=MESH,
        ).start()

    for_peers(send_a)
    keep_a = pltpu.make_async_copy(outbox.at[i], inbox.at[i], local_sem.at[2])
    keep_a.start()

    halos = []
    for n, (part, first, dst, to) in enumerate(((lw_prev, 8, 1, next_k), (lw_next, 0, 2, prev_k))):
        halos.append(
            pltpu.make_async_remote_copy(
                src_ref=weight.at[:, pl.ds(first, 8), pl.ds(block, 16), :],
                dst_ref=part,
                send_sem=halo_send.at[2 * n],
                recv_sem=halo_recv.at[2 * n],
                device_id={"colat": to},
                device_id_type=MESH,
            )
        )
        halos.append(
            pltpu.make_async_remote_copy(
                src_ref=tapsbox.at[0],
                dst_ref=tapsbox.at[dst],
                send_sem=halo_send.at[2 * n + 1],
                recv_sem=halo_recv.at[2 * n + 1],
                device_id={"colat": to},
                device_id_type=MESH,
            )
        )
    for copy in halos:
        copy.start()

    tab[pl.ds(nops8, tab.shape[0] - nops8), :] = jnp.zeros((tab.shape[0] - nops8, theta), F32)
    load_table.wait()
    ops_pad = tab.shape[0] // 8
    for part in range(8):
        hi, lo = split(tab[pl.ds(part, ops_pad, stride=8), :])
        tcat_hi[:, part * theta : (part + 1) * theta] = hi
        tcat_lo[:, part * theta : (part + 1) * theta] = lo
    n = iota((128, 8 * theta), 0)
    x = iota((128, 8 * theta), 1)
    match = ((x & (theta - 1)) == 16 * k + (n & 15)) & (x // theta == n >> 4)
    choose = ones_where(match).astype(BF16)
    tab_t[:, :ops_pad] = dot_nt(choose, tcat_hi[...]).astype(BF16)
    tab_t[:, ops_pad:] = dot_nt(choose, tcat_lo[...]).astype(BF16)
    for ref, index in ((wide_ops, ops), (wide_partners, partners)):
        index = index[...]
        ref[...] = jnp.concatenate([index, index[:, 128:]], axis=1)

    rows = [iota((r, 16, 256), 0) * 16 + iota((r, 16, 256), 1) for r in (16, ops_pad // 16 - 16)]
    rows = [r.astype(F32).astype(BF16) for r in rows]

    def hot(index, rows):
        index = jnp.broadcast_to(index, (16, 256)).astype(F32).astype(BF16)
        mask = rows == index[None]
        return jnp.where(mask, jnp.ones((), BF16), jnp.zeros((), BF16)).reshape(-1, 256)

    def gather_factors(p, carry):
        op = wide_ops[pl.ds(p, 1), :]
        first, second = hot(op, rows[0]), hot(op - 256, rows[1])
        factors[p] = dot(tab_t[...], jnp.concatenate([first, second, first, second], axis=0))
        partner = wide_partners[pl.ds(p, 1), :]
        picks[p] = hot((partner & 1) * 128 + (partner >> 1), rows[0])
        return carry

    lax.fori_loop(0, npart, gather_factors, 0, unroll=2)

    load_lw.wait()
    for copy in halos:
        copy.wait_recv()
    phi_lane = 4 * lax.rem(i, 4)
    users = weight.shape[3]
    folded = jnp.zeros((128, users), F32)
    for part, (box, first, offset, rows) in enumerate(
        ((lw_own, 0, 0, 16), (lw_prev, 8, -16, 8), (lw_next, 0, 16, 8))
    ):
        hi, lo = band(tapsbox[part], first, offset, rows, phi_lane)
        leaf = box[...].reshape(32 * rows, users)
        term = dot(hi, leaf) + dot(lo, leaf)
        if part == 1:
            term = jnp.where(k > 0, term, 0.0)
        if part == 2:
            term = jnp.where(k < colat - 1, term, 0.0)
        folded = folded + term
    fold_hi, fold_lo = split(folded.T)
    fold[...] = jnp.concatenate([fold_hi, fold_hi, fold_lo], axis=1)

    gbd_hi[...] = jnp.zeros(gbd_hi.shape, BF16)
    gbd_lo[...] = jnp.zeros(gbd_lo.shape, BF16)
    rcat[...] = jnp.zeros(rcat.shape, BF16)
    slots = returns.shape[0]
    listed = jnp.concatenate([returns[...], jnp.zeros((slots, 128 - lon), I32)], axis=1)
    listed = jnp.concatenate([listed, jnp.zeros((128 - slots, 128), I32)], axis=0).astype(F32).T
    for r in range(slots):
        column = listed[:lon, r : r + 1].astype(I32)
        ohret[:, r * 256 : (r + 1) * 256] = ones_where(iota((lon, 256), 1) == column).astype(BF16)

    xn = iota((256, 256), 0)
    xk = iota((256, 256), 1)
    phi = ((xk >> 7) & 1) * 2 + ((xk >> 6) & 1)
    match = (
        ((xk & 15) == (xn & 15))
        & (phi == ((xn >> 4) & 3))
        & (((xk >> 4) & 1) == ((xn >> 6) & 1))
        & (((xk >> 5) & 1) == (xn >> 7))
    )
    place[...] = ones_where(match).astype(BF16)
    keep_a.wait()
    pltpu.make_async_copy(inbox.at[pl.ds(0, lon - 1)], inbox.at[pl.ds(0, lon - 1)], a_recv).wait()
    rcat[:lon, :] = jnp.concatenate([inbox[:, 0, :], inbox[:, 1, :]], axis=1).astype(BF16)
    columns = dot_nt(place[...], rcat[...]).astype(BF16)
    src[:, :128] = columns[:128]
    src[:, 128:] = columns[128:]

    acc[...] = jnp.zeros(acc.shape, F32)

    def translate(g, carry):
        real = jnp.zeros((64, 256), F32)
        imag = jnp.zeros((64, 256), F32)
        for q in range(STEP):
            s = dot(src[...], picks[STEP * g + q])
            f = factors[STEP * g + q]
            real = real + (f[:64] * s[:64] - f[64:] * s[64:])
            imag = imag + (f[:64] * s[64:] + f[64:] * s[:64])
        acc[:64, :] += real
        acc[64:, :] += imag
        return carry

    lax.fori_loop(0, npart // STEP, translate, 0)
    t_hi, t_lo = split(acc[...])
    partial = dot(fold[...], jnp.concatenate([t_hi, t_lo, t_hi], axis=0))

    for c in range(colat):
        mine = partial[c * UC : (c + 1) * UC, :]
        tail = jnp.where(iota((16, 128), 1) < 64, mine[:16, 128:], mine[16:, 128:])
        rs_out[c] = jnp.concatenate([mine[:, :128], tail], axis=0).astype(BF16)

    def send_rs(s, carry):
        to = lax.rem(k + s, colat)
        pltpu.make_async_remote_copy(
            src_ref=rs_out.at[to],
            dst_ref=rs_in.at[k],
            send_sem=rs_send,
            recv_sem=rs_recv,
            device_id={"colat": to},
            device_id_type=MESH,
        ).start()
        return carry

    lax.fori_loop(1, colat, send_rs, 0)
    keep_rs = pltpu.make_async_copy(rs_out.at[k], rs_in.at[k], local_sem.at[3])
    keep_rs.start()
    keep_rs.wait()
    pltpu.make_async_copy(rs_in.at[pl.ds(0, colat - 1)], rs_in.at[pl.ds(0, colat - 1)], rs_recv).wait()
    total = rs_in[0].astype(F32)
    for c in range(1, colat):
        total = total + rs_in[c].astype(F32)
    tail = jnp.concatenate([total[UC:, :], pltpu.roll(total[UC:, :], 64, 1)], axis=0)
    tail = jnp.where(iota((UC, 128), 1) < 64, tail, 0.0)
    g_hi, g_lo = split(jnp.concatenate([total[:UC, :], tail], axis=1))
    for r in range(4):
        gbd_hi[r * UC : (r + 1) * UC, r * 256 : (r + 1) * 256] = g_hi
        gbd_lo[r * UC : (r + 1) * UC, r * 256 : (r + 1) * 256] = g_lo
    outbox2[:, 0, :] = dot_nt(ohret[:, :1024], gbd_hi[...]) + dot_nt(ohret[:, :1024], gbd_lo[...])
    outbox2[:, 1, :] = dot_nt(ohret[:, 1024:], gbd_hi[:, :256]) + dot_nt(ohret[:, 1024:], gbd_lo[:, :256])

    def send_b(to):
        pltpu.make_async_remote_copy(
            src_ref=outbox2.at[to],
            dst_ref=inbox2.at[i],
            send_sem=b_send,
            recv_sem=b_recv,
            device_id={"lon": to},
            device_id_type=MESH,
        ).start()

    for_peers(send_b)
    keep_b = pltpu.make_async_copy(outbox2.at[i], inbox2.at[i], local_sem.at[4])
    keep_b.start()
    keep_b.wait()
    pltpu.make_async_copy(inbox2.at[pl.ds(0, lon - 1)], inbox2.at[pl.ds(0, lon - 1)], b_recv).wait()
    field = jnp.sum(inbox2[...], axis=0)
    result = jnp.concatenate([field[0:1, r * UC : (r + 1) * UC] for r in range(4)] + [field[1:2, :UC]], axis=0)
    out[:, 0, :] = jnp.where(iota((slots, UC), 0) < count[0], result, 0.0)

    for copy in halos:
        copy.wait_send()
    pltpu.make_async_copy(outbox.at[pl.ds(0, lon - 1)], outbox.at[pl.ds(0, lon - 1)], a_send).wait()
    pltpu.make_async_copy(rs_out.at[pl.ds(0, colat - 1)], rs_out.at[pl.ds(0, colat - 1)], rs_send).wait()
    pltpu.make_async_copy(outbox2.at[pl.ds(0, lon - 1)], outbox2.at[pl.ds(0, lon - 1)], b_send).wait()


def body(
    lon,
    colat,
    pattern,
    phi_filter,
    trans_table,
    partners,
    op_index,
    anter_weight,
    return_boxes,
    return_count,
    leaf_weight,
):
    nops, _, theta, _ = trans_table.shape
    npart, nbox = partners.shape[1], partners.shape[0]
    slots = return_boxes.shape[1]
    phi = phi_filter.shape[0]
    users = leaf_weight.shape[3]
    ops_pad = -(-nops // 128) * 128
    vmem, hbm = pl.BlockSpec(memory_space=pltpu.VMEM), pl.BlockSpec(memory_space=pl.ANY)
    smem = pl.BlockSpec(memory_space=pltpu.SMEM)
    return pl.pallas_call(
        functools.partial(kernel, lon, colat),
        out_shape=jax.ShapeDtypeStruct((slots, 1, users // colat), F32),
        in_specs=[hbm, hbm, hbm, hbm, hbm, hbm, smem, hbm, hbm],
        out_specs=vmem,
        scratch_shapes=[
            pltpu.VMEM((pattern.size // phi, phi), BF16),
            pltpu.VMEM((phi, phi), BF16),
            pltpu.VMEM((npart, nbox), I32),
            pltpu.VMEM((npart, nbox), I32),
            pltpu.VMEM(anter_weight.shape[::-1], F32),
            pltpu.VMEM(return_boxes.shape[::-1], I32),
            pltpu.VMEM((lon, 2, 128), F32),
            pltpu.VMEM((lon, 2, 128), F32),
            pltpu.VMEM((phi, 128), F32),
            pltpu.VMEM((ops_pad * 8, theta), F32),
            pltpu.VMEM((ops_pad, 8 * theta), BF16),
            pltpu.VMEM((ops_pad, 8 * theta), BF16),
            pltpu.VMEM((128, 2 * ops_pad), BF16),
            pltpu.VMEM((128, 256), BF16),
            pltpu.VMEM((256, 256), BF16),
            pltpu.VMEM((users, 384), BF16),
            pltpu.VMEM((npart, 256), I32),
            pltpu.VMEM((npart, 256), I32),
            pltpu.VMEM((128, 256), BF16),
            pltpu.VMEM((npart, 128, 256), F32),
            pltpu.VMEM((npart, 256, 256), BF16),
            pltpu.VMEM((2, 16, 16, users), BF16),
            pltpu.VMEM((2, 8, 16, users), BF16),
            pltpu.VMEM((2, 8, 16, users), BF16),
            pltpu.VMEM((3, 16, 128), F32),
            pltpu.VMEM((128, 256), F32),
            pltpu.VMEM((colat, RS_ROWS, 128), BF16),
            pltpu.VMEM((colat, RS_ROWS, 128), BF16),
            pltpu.VMEM((128, 1024), BF16),
            pltpu.VMEM((128, 1024), BF16),
            pltpu.VMEM((lon, slots * 256), BF16),
            pltpu.VMEM((lon, 2, 128), F32),
            pltpu.VMEM((lon, 2, 128), F32),
            pltpu.SemaphoreType.DMA((6,)),
            pltpu.SemaphoreType.DMA((5,)),
            pltpu.SemaphoreType.DMA((4,)),
            pltpu.SemaphoreType.DMA((4,)),
            pltpu.SemaphoreType.DMA,
            pltpu.SemaphoreType.DMA,
            pltpu.SemaphoreType.DMA,
            pltpu.SemaphoreType.DMA,
            pltpu.SemaphoreType.DMA,
            pltpu.SemaphoreType.DMA,
        ],
        compiler_params=pltpu.CompilerParams(
            collective_id=0, has_side_effects=True, vmem_limit_bytes=60 * 1024 * 1024
        ),
        name="mlfma_pass",
    )(
        pattern.reshape(-1, phi),
        phi_filter,
        partners.T,
        op_index.T,
        anter_weight.T,
        return_boxes.T,
        return_count,
        trans_table.transpose(0, 1, 3, 2).reshape(nops * 8, theta),
        leaf_weight,
    ).transpose(1, 0, 2)


def solution(mesh):
    in_specs = (
        P("lon", None, "colat", None),
        P(),
        P(None, None, None, "lon"),
        P(),
        P(),
        P(None, "colat"),
        P(),
        P("lon"),
        P(None, "colat", None, None),
    )
    out_specs = P("lon", None, "colat")
    run = functools.partial(body, mesh.shape["lon"], mesh.shape["colat"])
    return jax.shard_map(run, mesh=mesh, in_specs=in_specs, out_specs=out_specs, check_vma=False)
```

profile of v0, /device:TPU:1, one launch (start us, length us, event | category | flops | bytes accessed | tf_op | source)
XLA Modules:
  0.0 49.7 jit_solution(1131777464037651494)
XLA Ops:
  0.7 47.8 %mlfma_pass.1 = f32[5,1,32]{2,1,0:T(1,128)} custom-call(bf16[64,384]{1,0:T(8,128)(2,1)} %bitcast.10, bf16[384,384]{1,0:T(8,128)(2,1)} %phi_filter_hbm.1, s32[40,192]{1,0:T(8,128)} %bitcast.11, s32[40,192]{1,0:T(8,128)} %bitcast.12, f32[16,17]{1,0:T(8,128)} %bitcast.14, s32[5,96]{1,0:T(8,128)} %bitcast.15, s32[1]{0:T(128)S(6)} %copy.11.count, ...), custom_call_target="tpu_custom_call" | custom-call | tf_op jit(solution)/shard_map/mlfma_pass/pallas_call | solution.py:408
  48.5 1.3 %copy.12 = f32[1,5,32]{2,0,1:T(1,128)} copy(f32[1,5,32]{2,0,1:T(1,128)} %bitcast.13) | data formatting | bytes 1280
where the time goes:
time: 49.9 us; the launch traced here: 49.7 us
  Pallas kernels  47.8 us (96%)
  local copies, waits for them, and re-layouts  1.26 us (3%)
  between operations  0.66 us (1%)
    pallas_call x1, Pallas kernels, body(): pl.pallas_call(functools.partial(kernel, lon, colat), out_shape=jax.Shape...  47.8 us
    unnamed x1, local copies, waits for them, and re-layouts  1.26 us

commit v1 on v0

--- a/solution.py
+++ b/solution.py
@@ -63,7 +63,7 @@
     ops_hbm,
     taps_hbm,
     returns_hbm,
-    count,
+    count_hbm,
     table,
     weight,
     out,
@@ -73,6 +73,7 @@
     ops,
     taps,
     returns,
+    count,
     outbox,
     inbox,
     ybuf,
@@ -160,6 +161,7 @@
                 (ops_hbm, ops),
                 (partners_hbm, partners),
                 (returns_hbm, returns),
+                (count_hbm, count),
             )
         )
     ]
@@ -404,11 +406,10 @@
     users = leaf_weight.shape[3]
     ops_pad = -(-nops // 128) * 128
     vmem, hbm = pl.BlockSpec(memory_space=pltpu.VMEM), pl.BlockSpec(memory_space=pl.ANY)
-    smem = pl.BlockSpec(memory_space=pltpu.SMEM)
     return pl.pallas_call(
         functools.partial(kernel, lon, colat),
         out_shape=jax.ShapeDtypeStruct((slots, 1, users // colat), F32),
-        in_specs=[hbm, hbm, hbm, hbm, hbm, hbm, smem, hbm, hbm],
+        in_specs=[hbm] * 6 + [pl.BlockSpec(memory_space=pltpu.HBM)] + [hbm] * 2,
         out_specs=vmem,
         scratch_shapes=[
             pltpu.VMEM((pattern.size // phi, phi), BF16),
@@ -417,6 +418,7 @@
             pltpu.VMEM((npart, nbox), I32),
             pltpu.VMEM(anter_weight.shape[::-1], F32),
             pltpu.VMEM(return_boxes.shape[::-1], I32),
+            pltpu.SMEM((1,), I32),
             pltpu.VMEM((lon, 2, 128), F32),
             pltpu.VMEM((lon, 2, 128), F32),
             pltpu.VMEM((phi, 128), F32),
@@ -444,7 +446,7 @@
             pltpu.VMEM((lon, slots * 256), BF16),
             pltpu.VMEM((lon, 2, 128), F32),
             pltpu.VMEM((lon, 2, 128), F32),
-            pltpu.SemaphoreType.DMA((6,)),
+            pltpu.SemaphoreType.DMA((7,)),
             pltpu.SemaphoreType.DMA((5,)),
             pltpu.SemaphoreType.DMA((4,)),
             pltpu.SemaphoreType.DMA((4,)),

time: 49.9 us -> 50 us (level)
  no operation moved by 1% of the time
where the time goes in v1:
time: 50 us; the launch traced here: 49.8 us
  Pallas kernels  47.9 us (96%)
  local copies, waits for them, and re-layouts  1.26 us (3%)
  between operations  0.66 us (1%)
    pallas_call x1, Pallas kernels, body(): pl.pallas_call(functools.partial(kernel, lon, colat), out_shape=jax.Shape...  47.9 us
    unnamed x1, local copies, waits for them, and re-layouts  1.26 us

profile of v1, /device:TPU:1, one launch (start us, length us, event | category | flops | bytes accessed | tf_op | source)
XLA Modules:
  0.0 49.8 jit_solution(8582367358595670823)
XLA Ops:
  0.7 47.9 %mlfma_pass.1 = f32[5,1,32]{2,1,0:T(1,128)} custom-call(bf16[64,384]{1,0:T(8,128)(2,1)} %bitcast.10, bf16[384,384]{1,0:T(8,128)(2,1)} %phi_filter_hbm.1, s32[40,192]{1,0:T(8,128)} %bitcast.11, s32[40,192]{1,0:T(8,128)} %bitcast.12, f32[16,17]{1,0:T(8,128)} %bitcast.14, s32[5,96]{1,0:T(8,128)} %bitcast.15, s32[1]{0:T(128)S(6)} %copy.11.count_hbm, ...), custom_call_target="tpu_custom_call" | custom-call | tf_op jit(solution)/shard_map/mlfma_pass/pallas_call | solution.py:409
  48.5 1.3 %copy.12 = f32[1,5,32]{2,0,1:T(1,128)} copy(f32[1,5,32]{2,0,1:T(1,128)} %bitcast.13) | data formatting | bytes 1280
